TPU v7x, 512 devices: a whole 4x4x16 slice. The times are simulated.
512 devices in a mesh: replica: 32 (over z, y_lo), fsdp: 16 (over x, y_hi, core).
Axes of the slice: x: 4, y: 4 (y_hi: 2, y_lo: 2; y = y_hi * 2 + y_lo), z: 16, core: 2. Of those that a mesh axis runs over, the one named last changes fastest.
Arguments:
- tokens: bfloat16 [32, 2048, 4096], P('replica', 'fsdp'), may hold values from -6 to 6
- local_weight: bfloat16 [32, 4096, 512], P('replica', 'fsdp'), may hold values from -6 to 6
- key_cot: bfloat16 [32, 2048, 512], P('replica', 'fsdp'), may hold values from -6 to 6
- global_weight: float32 [4096, 512], P(('fsdp', 'replica')), may hold values from -6 to 6
- momentum: float32 [4096, 512], P(('fsdp', 'replica')), may hold values from -6 to 6
- anchor: float32 [4096, 512], P(('fsdp', 'replica')), may hold values from -6 to 6
Outputs:
- keys: bfloat16 [32, 2048, 512], P('replica', 'fsdp')
- grad_tokens: bfloat16 [32, 2048, 4096], P('replica', 'fsdp')
- grad_weight: bfloat16 [32, 4096, 512], P('replica', 'fsdp')
- momentum_new: float32 [4096, 512], P(('fsdp', 'replica'))
- global_new: float32 [4096, 512], P(('fsdp', 'replica'))
- synced: bfloat16 [4096, 512], P('fsdp')
All inputs are finite; a program needn't handle non-finite values.
Results may differ from a plain program's by a relative error of at most 0.0095.
Values may be sent and summed in bfloat16 or wider, within the bound.
A program may use at most 64 MiB of HBM per device.

v0:
```python
import jax
import jax.numpy as jnp
from jax import lax
from jax.sharding import PartitionSpec as P

D_WIN = 4096


def on_device(tokens, local_weight, key_cot, global_weight, momentum, anchor):
    scale = 1.0 / D_WIN**0.5
    inputs = tokens[0]
    weight = local_weight[0]
    cot = key_cot[0]
    total = lax.psum_scatter(
        weight.astype(jnp.float32).astype(jnp.bfloat16), "replica", scatter_dimension=0, tiled=True
    ).astype(jnp.float32)
    pseudo = global_weight - total / lax.axis_size("replica")
    push = pseudo + 0.1 * (global_weight - anchor)
    momentum_new = 0.9 * momentum + push
    global_new = global_weight - 0.7 * (push + 0.9 * momentum_new)
    synced = lax.all_gather(global_new.astype(jnp.bfloat16), "replica", axis=0, tiled=True)
    columns_all = lax.all_to_all(inputs, "fsdp", split_axis=1, concat_axis=0, tiled=True)
    cot_all = lax.all_gather(cot, "fsdp", axis=0, tiled=True)
    wgrad = lax.dot_general(
        columns_all, cot_all, (((0,), (0,)), ((), ())), preferred_element_type=jnp.float32
    )
    grad_weight = (wgrad * scale).astype(jnp.bfloat16)
    piece = lax.all_gather(weight, "fsdp", axis=0, tiled=True)
    key_total = jnp.dot(inputs, piece, preferred_element_type=jnp.float32)
    part = lax.dot_general(cot, piece, (((1,), (1,)), ((), ())), preferred_element_type=jnp.float32)
    back_full = part
    summed, back_full = (key_total, back_full)
    keys = (summed * scale).astype(jnp.bfloat16)
    grad_tokens = (back_full * scale).astype(jnp.bfloat16)
    return (keys[None], grad_tokens[None], grad_weight[None], momentum_new, global_new, synced)


def solution(mesh):
    in_specs = (
        P("replica", "fsdp", None),
        P("replica", "fsdp", None),
        P("replica", "fsdp", None),
        P(("fsdp", "replica"), None),
        P(("fsdp", "replica"), None),
        P(("fsdp", "replica"), None),
    )
    out_specs = (
        P("replica", "fsdp", None),
        P("replica", "fsdp", None),
        P("replica", "fsdp", None),
        P(("fsdp", "replica"), None),
        P(("fsdp", "replica"), None),
        P("fsdp", None),
    )
    return jax.shard_map(
        on_device, mesh=mesh, in_specs=in_specs, out_specs=out_specs, check_vma=False
    )
```

profile of v0, /device:TPU:16, one launch (start us, length us, event | category | flops | bytes accessed | tf_op | source)
XLA Modules:
  0.0 245.4 jit_solution(13214008306867970524)
XLA Ops:
  8.0 0.0 copy-start.3
  8.0 0.0 copy-start.4
  8.0 0.0 copy-start.5
  8.0 0.0 reduce-scatter.2.cloned.1.call-start
  8.1 0.7 reduce-scatter.2.cloned.1.call-update
  8.8 0.0 all-gather.7.cloned.1.call-start
  8.8 0.5 all-gather.7.cloned.1.call-update
  9.3 0.0 all-gather.5.cloned.1.call-start
  9.4 0.5 all-gather.5.cloned.1.call-update
  9.9 2.3 copy.12
  12.2 0.0 copy-start.1
  12.2 9.3 %all-to-all-start = ((bf16[128,16,256]{0,2,1:T(8,128)(2,1)}), bf16[128,16,256]{0,2,1:T(8,128)(2,1)S(1)}, u32[]{:S(2)}, u32[]{:S(2)}) async-start(bf16[128,16,256]{0,2,1:T(8,128)(2,1)} %bitcast.5), calls=%async_computation | async-start | bytes 2097152 | tf_op jit(solution)/shard_map/all_to_all | solution.py:22
  21.5 142.5 %reduce-scatter.2.cloned.1.call-done = bf16[8,512]{1,0:T(8,128)(2,1)} async-done(((bf16[256,512]{1,0:T(8,128)(2,1)}), bf16[8,512]{1,0:T(8,128)(2,1)}) %reduce-scatter.2.cloned.1.call-update) | async-done | bytes 8208 | tf_op jit(solution)/shard_map/reduce_scatter | solution.py:14
  164.0 0.0 copy-done.3
  164.0 0.0 copy-done.4
  164.0 0.0 copy-done.5
  164.0 1.3 fusion.27
  165.4 62.1 %all_gather.11 = bf16[256,512]{1,0:T(8,128)(2,1)S(1)} all-gather(bf16[8,512]{1,0:T(8,128)(2,1)S(1)} %get-tuple-element.6), channel_id=1, replica_groups=mesh['replica'=32,'fsdp'=16] {'replica'}, dimensions={0}, use_global_device_ids=true | all-gather | bytes 270336 | tf_op jit(solution)/shard_map/all_gather | solution.py:21
  227.4 0.0 all-to-all-done
  227.4 0.5 copy.13
  228.0 0.0 all-gather.7.cloned.1.call-done
  228.0 0.0 copy-start.2
  228.0 3.1 %fusion.13 = bf16[1,256,512]{2,1,0:T(8,128)(2,1)} fusion(bf16[2048,256]{1,0:T(8,128)(2,1)S(1)} %bitcast.38, bf16[1,2048,512]{2,1,0:T(8,128)(2,1)} %all-gather.7.cloned.1.call-done), kind=kOutput, calls=%fused_computation.10 | convolution fusion | flops 537133056 | bytes 3407872 | tf_op jit(solution)/shard_map/dot_general | solution.py:24
  231.1 0.0 all-gather.5.cloned.1.call-done
  231.1 0.0 copy-done.1
  231.1 0.0 copy-start
  231.1 3.7 %fusion.22 = bf16[1,128,512]{2,1,0:T(8,128)(2,1)} fusion(bf16[1,4096,512]{2,1,0:T(8,128)(2,1)} %all-gather.5.cloned.1.call-done, bf16[1,128,4096]{2,1,0:T(8,128)(2,1)S(1)} %copy-done.1), kind=kOutput, calls=%fused_computation.13 | convolution fusion | flops 537001984 | bytes 5373952 | tf_op jit(solution)/shard_map/dot_general | solution.py:29
  234.8 0.0 copy-done.2
  234.8 0.0 copy-done
  234.8 2.5 %fusion.1 = bf16[1,128,4096]{2,1,0:T(8,128)(2,1)} fusion(bf16[1,4096,512]{2,1,0:T(8,128)(2,1)S(1)} %copy-done, bf16[1,128,512]{2,1,0:T(8,128)(2,1)S(1)} %copy-done.2), kind=kOutput, calls=%fused_computation.2 | convolution fusion | flops 537919488 | bytes 5373952 | tf_op jit(solution)/shard_map/dot_general | solution.py:30
  237.2 0.7 copy.15
Async XLA Ops:
  8.0 156.0 %copy-start.3 = (f32[8,512]{1,0:T(8,128)S(1)}, f32[8,512]{1,0:T(8,128)}, u32[]{:S(2)}) copy-start(f32[8,512]{1,0:T(8,128)} %param.9) | copy-start | bytes 49156
  8.0 156.0 %copy-start.4 = (f32[8,512]{1,0:T(8,128)S(1)}, f32[8,512]{1,0:T(8,128)}, u32[]{:S(2)}) copy-start(f32[8,512]{1,0:T(8,128)} %param.11) | copy-start | bytes 49156
  8.0 156.0 %copy-start.5 = (f32[8,512]{1,0:T(8,128)S(1)}, f32[8,512]{1,0:T(8,128)}, u32[]{:S(2)}) copy-start(f32[8,512]{1,0:T(8,128)} %param.10) | copy-start | bytes 49156
  8.0 156.0 %reduce-scatter.2.cloned.1.call-start = ((), (), s32[]{:S(2)}) async-start(), calls=%async_computation.2 | async-start | bytes 270336 | tf_op jit(solution)/shard_map/reduce_scatter | solution.py:14
  8.8 219.2 %all-gather.7.cloned.1.call-start = ((), (), s32[]{:S(2)}) async-start(), calls=%async_computation.4 | async-start | bytes 2228224 | tf_op jit(solution)/shard_map/all_gather | solution.py:23
  9.3 221.7 %all-gather.5.cloned.1.call-start = ((), (), s32[]{:S(2)}) async-start(), calls=%async_computation.3 | async-start | bytes 4456448 | tf_op jit(solution)/shard_map/all_gather | solution.py:28
  12.2 218.9 %copy-start.1 = (bf16[1,128,4096]{2,1,0:T(8,128)(2,1)S(1)}, bf16[1,128,4096]{2,1,0:T(8,128)(2,1)}, u32[]{:S(2)}) copy-start(bf16[1,128,4096]{2,1,0:T(8,128)(2,1)} %param.6) | copy-start | bytes 3145732
  12.2 215.2 %all-to-all-start = ((bf16[128,16,256]{0,2,1:T(8,128)(2,1)}), bf16[128,16,256]{0,2,1:T(8,128)(2,1)S(1)}, u32[]{:S(2)}, u32[]{:S(2)}) async-start(bf16[128,16,256]{0,2,1:T(8,128)(2,1)} %bitcast.5), calls=%async_computation | async-start | bytes 2097152 | tf_op jit(solution)/shard_map/all_to_all | solution.py:22
  228.0 6.8 %copy-start.2 = (bf16[1,128,512]{2,1,0:T(8,128)(2,1)S(1)}, bf16[1,128,512]{2,1,0:T(8,128)(2,1)}, u32[]{:S(2)}) copy-start(bf16[1,128,512]{2,1,0:T(8,128)(2,1)} %param.8) | copy-start | bytes 393220
  231.1 3.7 %copy-start = (bf16[1,4096,512]{2,1,0:T(8,128)(2,1)S(1)}, bf16[1,4096,512]{2,1,0:T(8,128)(2,1)}, u32[]{:S(2)}) copy-start(bf16[1,4096,512]{2,1,0:T(8,128)(2,1)} %all-gather.5.cloned.1.call-done) | copy-start | bytes 12582916
Sparse Core Ops, SparseCore 0:
  11.6 152.3 reduce-scatter.1
Sparse Core Ops, SparseCore 1:
  12.5 65.7 all-gather.6
  81.4 71.1 all-gather.4
where the time goes:
time: 246 us; the launch traced here: 245 us
  waiting for transfers between devices  144 us (59%)
  blocking collectives  62.1 us (25%)
  between operations  15.5 us (6%)
  starting transfers between devices  9.41 us (4%)
  matrix products  9.23 us (4%)
  local copies, waits for them, and re-layouts  3.52 us (1%)
    reduce_scatter x1, waiting for transfers between devices, on_device(): lax.psum_scatter(weight.astype(jnp.float32).astype(jnp.bfloat16), 'replic...  143 us
    all_gather x1, blocking collectives, on_device(): lax.all_gather(global_new.astype(jnp.bfloat16), 'replica', axis=0, tiled=...  62.1 us
    all_to_all x1, starting transfers between devices, on_device(): lax.all_to_all(inputs, 'fsdp', split_axis=1, concat_axis=0, tiled=True)  9.29 us
  transfers between devices with their start and end apart: 4, of which 1 were waited for; matrix products, arithmetic and copies ran while one was open for 3% of the time, Pallas kernels for 0%

commit v1 on v0

--- a/solution.py
+++ b/solution.py
@@ -18,7 +18,12 @@
     push = pseudo + 0.1 * (global_weight - anchor)
     momentum_new = 0.9 * momentum + push
     global_new = global_weight - 0.7 * (push + 0.9 * momentum_new)
-    synced = lax.all_gather(global_new.astype(jnp.bfloat16), "replica", axis=0, tiled=True)
+    synced = jnp.concatenate(
+        lax.all_to_all(
+            jnp.stack([global_new.astype(jnp.bfloat16)] * lax.axis_size("replica")), "replica", 0, 0
+        ),
+        axis=0,
+    )
     columns_all = lax.all_to_all(inputs, "fsdp", split_axis=1, concat_axis=0, tiled=True)
     cot_all = lax.all_gather(cot, "fsdp", axis=0, tiled=True)
     wgrad = lax.dot_general(

time: 246 us -> 211 us (0.86)
  the two profiles are of different devices: /device:TPU:16 before, /device:TPU:4 now
where the time goes in v1:
time: 211 us; the launch traced here: 210 us
  waiting for transfers between devices  159 us (75%)
  starting transfers between devices  20.7 us (10%)
  between operations  15.5 us (7%)
  matrix products  9.23 us (4%)
  local copies, waits for them, and re-layouts  4.24 us (2%)
    reduce_scatter x1, waiting for transfers between devices, on_device(): lax.psum_scatter(weight.astype(jnp.float32).astype(jnp.bfloat16), 'replic...  140 us
    all_to_all x1, waiting for transfers between devices, on_device(): lax.all_to_all(jnp.stack([global_new.astype(jnp.bfloat16)] * lax.axis_siz...  17.2 us
    all_to_all x1, starting transfers between devices, on_device(): lax.all_to_all(jnp.stack([global_new.astype(jnp.bfloat16)] * lax.axis_siz...  11.1 us
    all_to_all x1, starting transfers between devices, on_device(): lax.all_to_all(inputs, 'fsdp', split_axis=1, concat_axis=0, tiled=True)  9.5 us
  transfers between devices with their start and end apart: 5, of which 2 were waited for; matrix products, arithmetic and copies ran while one was open for 4% of the time, Pallas kernels for 0%

profile of v1, /device:TPU:4, one launch (start us, length us, event | category | flops | bytes accessed | tf_op | source)
XLA Modules:
  0.0 210.3 jit_solution(3086566996455828983)
XLA Ops:
  8.0 0.0 copy-start.3
  8.0 0.0 copy-start.4
  8.0 0.0 copy-start.5
  8.0 0.0 reduce-scatter.2.cloned.1.call-start
  8.1 0.7 reduce-scatter.2.cloned.1.call-update
  8.8 0.0 all-gather.7.cloned.1.call-start
  8.8 0.5 all-gather.7.cloned.1.call-update
  9.3 0.0 all-gather.5.cloned.1.call-start
  9.4 0.5 all-gather.5.cloned.1.call-update
  9.9 2.3 %copy.12 = bf16[1,128,4096]{1,2,0:T(8,128)(2,1)} copy(bf16[1,128,4096]{2,1,0:T(8,128)(2,1)} %param.6) | data formatting | bytes 2097152 | tf_op args[0]
  12.2 0.0 copy-start.1
  12.2 9.5 %all-to-all-start = ((bf16[128,16,256]{0,2,1:T(8,128)(2,1)}), bf16[128,16,256]{0,2,1:T(8,128)(2,1)S(1)}, u32[]{:S(2)}, u32[]{:S(2)}) async-start(bf16[128,16,256]{0,2,1:T(8,128)(2,1)} %bitcast.5), calls=%async_computation | async-start | bytes 2097152 | tf_op jit(solution)/shard_map/all_to_all | solution.py:27
  21.7 140.2 %reduce-scatter.2.cloned.1.call-done = bf16[8,512]{1,0:T(8,128)(2,1)} async-done(((bf16[256,512]{1,0:T(8,128)(2,1)}), bf16[8,512]{1,0:T(8,128)(2,1)}) %reduce-scatter.2.cloned.1.call-update) | async-done | bytes 8208 | tf_op jit(solution)/shard_map/reduce_scatter | solution.py:14
  161.9 0.0 copy-done.3
  161.9 0.0 copy-done.4
  161.9 0.0 copy-done.5
  161.9 1.3 fusion.27
  163.3 0.0 all-to-all-done
  163.3 0.7 stack.2
  164.0 11.1 %all-to-all-start.1 = ((bf16[32,8,512]{2,1,0:T(8,128)(2,1)}), bf16[32,8,512]{2,1,0:T(8,128)(2,1)S(1)}, u32[]{:S(2)}, u32[]{:S(2)}) async-start(bf16[32,8,512]{2,1,0:T(8,128)(2,1)} %stack.2), calls=%async_computation.2 | async-start | bytes 524288 | tf_op jit(solution)/shard_map/all_to_all | solution.py:22
  175.1 0.5 copy.13
  175.7 17.2 %all-to-all-done.1 = bf16[32,8,512]{2,1,0:T(8,128)(2,1)S(1)} async-done(((bf16[32,8,512]{2,1,0:T(8,128)(2,1)}), bf16[32,8,512]{2,1,0:T(8,128)(2,1)S(1)}, u32[]{:S(2)}, u32[]{:S(2)}) %all-to-all-start.1) | async-done | bytes 262176 | tf_op jit(solution)/shard_map/all_to_all | solution.py:22
  192.9 0.0 all-gather.7.cloned.1.call-done
  192.9 0.0 copy-start.2
  192.9 3.1 %fusion.13 = bf16[1,256,512]{2,1,0:T(8,128)(2,1)} fusion(bf16[2048,256]{1,0:T(8,128)(2,1)S(1)} %bitcast.39, bf16[1,2048,512]{2,1,0:T(8,128)(2,1)} %all-gather.7.cloned.1.call-done), kind=kOutput, calls=%fused_computation.10 | convolution fusion | flops 537133056 | bytes 3407872 | tf_op jit(solution)/shard_map/dot_general | solution.py:29
  195.9 0.0 all-gather.5.cloned.1.call-done
  195.9 0.0 copy-done.1
  195.9 0.0 copy-start
  195.9 3.7 %fusion.22 = bf16[1,128,512]{2,1,0:T(8,128)(2,1)} fusion(bf16[1,4096,512]{2,1,0:T(8,128)(2,1)} %all-gather.5.cloned.1.call-done, bf16[1,128,4096]{2,1,0:T(8,128)(2,1)S(1)} %copy-done.1), kind=kOutput, calls=%fused_computation.13 | convolution fusion | flops 537001984 | bytes 5373952 | tf_op jit(solution)/shard_map/dot_general | solution.py:34
  199.7 0.0 copy-done.2
  199.7 0.0 copy-done
  199.7 2.5 %fusion.1 = bf16[1,128,4096]{2,1,0:T(8,128)(2,1)} fusion(bf16[1,4096,512]{2,1,0:T(8,128)(2,1)S(1)} %copy-done, bf16[1,128,512]{2,1,0:T(8,128)(2,1)S(1)} %copy-done.2), kind=kOutput, calls=%fused_computation.2 | convolution fusion | flops 537919488 | bytes 5373952 | tf_op jit(solution)/shard_map/dot_general | solution.py:35
  202.1 0.7 copy.15
Async XLA Ops:
  8.0 153.9 %copy-start.3 = (f32[8,512]{1,0:T(8,128)S(1)}, f32[8,512]{1,0:T(8,128)}, u32[]{:S(2)}) copy-start(f32[8,512]{1,0:T(8,128)} %param.9) | copy-start | bytes 49156
  8.0 153.9 %copy-start.4 = (f32[8,512]{1,0:T(8,128)S(1)}, f32[8,512]{1,0:T(8,128)}, u32[]{:S(2)}) copy-start(f32[8,512]{1,0:T(8,128)} %param.11) | copy-start | bytes 49156
  8.0 153.9 %copy-start.5 = (f32[8,512]{1,0:T(8,128)S(1)}, f32[8,512]{1,0:T(8,128)}, u32[]{:S(2)}) copy-start(f32[8,512]{1,0:T(8,128)} %param.10) | copy-start | bytes 49156
  8.0 153.9 %reduce-scatter.2.cloned.1.call-start = ((), (), s32[]{:S(2)}) async-start(), calls=%async_computation.3 | async-start | bytes 270336 | tf_op jit(solution)/shard_map/reduce_scatter | solution.py:14
  8.8 184.1 %all-gather.7.cloned.1.call-start = ((), (), s32[]{:S(2)}) async-start(), calls=%async_computation.5 | async-start | bytes 2228224 | tf_op jit(solution)/shard_map/all_gather | solution.py:28
  9.3 186.6 %all-gather.5.cloned.1.call-start = ((), (), s32[]{:S(2)}) async-start(), calls=%async_computation.4 | async-start | bytes 4456448 | tf_op jit(solution)/shard_map/all_gather | solution.py:33
  12.2 183.7 %copy-start.1 = (bf16[1,128,4096]{2,1,0:T(8,128)(2,1)S(1)}, bf16[1,128,4096]{2,1,0:T(8,128)(2,1)}, u32[]{:S(2)}) copy-start(bf16[1,128,4096]{2,1,0:T(8,128)(2,1)} %param.6) | copy-start | bytes 3145732
  12.2 151.1 %all-to-all-start = ((bf16[128,16,256]{0,2,1:T(8,128)(2,1)}), bf16[128,16,256]{0,2,1:T(8,128)(2,1)S(1)}, u32[]{:S(2)}, u32[]{:S(2)}) async-start(bf16[128,16,256]{0,2,1:T(8,128)(2,1)} %bitcast.5), calls=%async_computation | async-start | bytes 2097152 | tf_op jit(solution)/shard_map/all_to_all | solution.py:27
  164.0 28.9 %all-to-all-start.1 = ((bf16[32,8,512]{2,1,0:T(8,128)(2,1)}), bf16[32,8,512]{2,1,0:T(8,128)(2,1)S(1)}, u32[]{:S(2)}, u32[]{:S(2)}) async-start(bf16[32,8,512]{2,1,0:T(8,128)(2,1)} %stack.2), calls=%async_computation.2 | async-start | bytes 524288 | tf_op jit(solution)/shard_map/all_to_all | solution.py:22
  192.9 6.8 %copy-start.2 = (bf16[1,128,512]{2,1,0:T(8,128)(2,1)S(1)}, bf16[1,128,512]{2,1,0:T(8,128)(2,1)}, u32[]{:S(2)}) copy-start(bf16[1,128,512]{2,1,0:T(8,128)(2,1)} %param.8) | copy-start | bytes 393220
  195.9 3.7 %copy-start = (bf16[1,4096,512]{2,1,0:T(8,128)(2,1)S(1)}, bf16[1,4096,512]{2,1,0:T(8,128)(2,1)}, u32[]{:S(2)}) copy-start(bf16[1,4096,512]{2,1,0:T(8,128)(2,1)} %all-gather.5.cloned.1.call-done) | copy-start | bytes 12582916
Sparse Core Ops, SparseCore 0:
  11.6 150.2 reduce-scatter.1
Sparse Core Ops, SparseCore 1:
  12.5 66.8 all-gather.6
  82.5 70.7 all-gather.4
